TPU v7x, 256 devices: a whole 4x4x8 slice. The times are simulated.
256 devices in a mesh: heads: 8 (over z), seq: 32 (over x, y, core).
Axes of the slice: x: 4, y: 4, z: 8, core: 2. Of those that a mesh axis runs over, the one named last changes fastest.
Arguments:
- request_embeddings: bfloat16 [65536, 4096], P('seq', 'heads'), may hold values from -72 to 72
- attended_content_pile: bfloat16 [2, 65536, 4096], P(None, 'seq', 'heads'), may hold values from -4 to 4
- softness_progression: float32 [8], replicated, may hold values from 0.5 to 2
- segment_partner_chart: int32 [8, 512], P('heads'), may hold values from 0 to 511, as said below
Outputs:
- attended: bfloat16 [65536, 4096], P('seq', 'heads')
- entropy: float32 [32, 512], P('heads', 'seq')
Inputs may be any that keep to these rules, and one draw needn't show every extreme that they name: Each row of segment_partner_chart is a permutation of the 512 blocks; block j is held by index j // 16 of seq. In each row, of the 16 query blocks of one index of seq, at most 1 are matched to blocks held by any one index of seq, and this count is reached.
All inputs are finite; a program needn't handle non-finite values.
Results may differ from a plain program's by a relative error of at most 0.0043.
Values may be sent and summed in bfloat16 or wider, within the bound.
A program may use at most 128 MiB of HBM per device.

v0:
```python
import math

import jax
import jax.numpy as jnp
from jax import lax
from jax.sharding import PartitionSpec as P

HEADS = 32
HEAD_DIM = 128
BLOCK = 128
GROUP_HEADS = 4
REFIT_REPEATS = 8


def merged(array, axis, combine):
    everything = jax.tree.map(lambda part: lax.all_gather(part, axis), array)
    first = jax.tree.map(lambda part: part[0], everything)

    def lap(k, so_far):
        return combine(so_far, jax.tree.map(lambda part: part[k], everything))

    return lax.fori_loop(1, lax.axis_size(axis), lap, first)


def merge_lse(first, second):
    highest = jnp.maximum(first[0], second[0])
    return (
        highest,
        first[1] * jnp.exp(first[0] - highest) + second[1] * jnp.exp(second[0] - highest),
    )


def stochastic_proportions(request_potentials, softness_progression):
    column_dual_variable = jnp.zeros((request_potentials.shape[1],), jnp.float32)
    source_dual_variable = jnp.zeros((request_potentials.shape[0],), jnp.float32)
    chilled_charge_array = request_potentials
    for repeat_ordinal in range(REFIT_REPEATS):
        chilled_charge_array = request_potentials / softness_progression[repeat_ordinal]
        source_dual_variable = -jax.nn.logsumexp(
            chilled_charge_array + column_dual_variable[None, :], axis=1
        )
        shifted = chilled_charge_array + source_dual_variable[:, None]
        col_max = jnp.max(shifted, axis=0)
        col_sum = jnp.sum(jnp.exp(shifted - col_max[None, :]), axis=0)
        merged_max, merged_sum = merged((col_max, col_sum), "seq", merge_lse)
        column_dual_variable = -(merged_max + jnp.log(merged_sum))
    return chilled_charge_array + source_dual_variable[:, None] + column_dual_variable[None, :]


def part_stats(queries_five, keys_five, values_five):
    scores = jnp.einsum(
        "mqgha,mkgha->mghqk", queries_five, keys_five, preferred_element_type=jnp.float32
    ) * HEAD_DIM ** (-0.5)
    row_max = jnp.max(scores, axis=-1)
    exponent = jnp.exp(scores - row_max[..., None])
    totals = jnp.sum(exponent, axis=-1)
    moments = jnp.sum(exponent * scores, axis=-1)
    weights = exponent.astype(jnp.bfloat16)
    numerator = jnp.einsum(
        "mghqk,mkgha->mqgha", weights, values_five, preferred_element_type=jnp.float32
    )
    return (numerator, row_max, totals, moments)


def combine_parts(local_part, matched_part, bias):
    numer_local, max_local, total_local, moment_local = local_part
    numer_matched, max_matched, total_matched, moment_matched = matched_part
    bias_wide = bias[:, :, None, None]
    shifted = max_matched + bias_wide
    moment_shift = moment_matched + bias_wide * total_matched
    joint = jnp.maximum(max_local, shifted)
    weight_local = jnp.exp(max_local - joint)
    weight_matched = jnp.exp(shifted - joint)
    denominator = total_local * weight_local + total_matched * weight_matched
    entropy_rows = (
        jnp.log(denominator)
        + joint
        - (moment_local * weight_local + moment_shift * weight_matched) / denominator
    )
    share_local = jnp.transpose(weight_local / denominator, (0, 3, 1, 2))[..., None]
    share_matched = jnp.transpose(weight_matched / denominator, (0, 3, 1, 2))[..., None]
    mixed = numer_local * share_local + numer_matched * share_matched
    return (mixed, jnp.mean(entropy_rows, axis=-1))


def take_blocks(kv_blocks, send_index, send_valid):
    picked = jnp.take(kv_blocks[:, :, :, 0], send_index[0].reshape(-1), axis=1)
    keep = send_valid[0].reshape(-1)[None, :, None, None]
    taken = [jnp.where(keep, picked, jnp.zeros_like(picked))]
    return jnp.stack(taken, axis=3)


def on_device(
    request_embeddings, attended_content_pile, softness_progression, segment_partner_chart
):
    seq_count = lax.axis_size("seq")
    seq_rank = lax.axis_index("seq")
    tokens_dev, local_width = request_embeddings.shape
    blocks_dev = tokens_dev // BLOCK
    capacity = (blocks_dev + seq_count - 1) // seq_count
    all_blocks = blocks_dev * seq_count
    group_width = GROUP_HEADS * HEAD_DIM
    groups_dev = local_width // group_width
    local_heads = groups_dev * GROUP_HEADS
    price_multiplier = 1.0 / (BLOCK * math.sqrt(HEAD_DIM * HEADS))
    query_sums = jnp.sum(
        request_embeddings.reshape(blocks_dev, BLOCK, local_width), axis=1, dtype=jnp.float32
    )
    key_sums = jnp.sum(
        attended_content_pile[0].reshape(blocks_dev, BLOCK, local_width), axis=1, dtype=jnp.float32
    )
    incomplete_price = jnp.dot(
        query_sums,
        lax.all_gather(key_sums, "seq", axis=0, tiled=True).T,
        precision=lax.Precision.HIGHEST,
    )
    request_potentials = lax.psum(incomplete_price * price_multiplier, "heads")
    mass_shipment_shares = stochastic_proportions(request_potentials, softness_progression)
    exponent_joint_density = mass_shipment_shares + math.log(all_blocks)
    owners = (segment_partner_chart // blocks_dev).reshape(groups_dev, seq_count, blocks_dev)
    offsets = (segment_partner_chart % blocks_dev).reshape(groups_dev, seq_count, blocks_dev)
    block_iota = jnp.arange(blocks_dev, dtype=jnp.int32)
    earlier = block_iota[:, None] > block_iota[None, :]
    same_owner = owners[:, :, :, None] == owners[:, :, None, :]
    ranks = jnp.sum(jnp.logical_and(same_owner, earlier[None, None]), axis=-1)
    slot_iota = jnp.arange(capacity, dtype=jnp.int32)
    chosen = jnp.logical_and(
        (owners == seq_rank)[:, :, None, :], ranks[:, :, None, :] == slot_iota[None, None, :, None]
    )
    send_index = jnp.sum(jnp.where(chosen, offsets[:, :, None, :], 0), axis=-1)
    send_valid = jnp.any(chosen, axis=-1)
    own_owner = lax.dynamic_index_in_dim(owners, seq_rank, 1, keepdims=False)
    own_rank = lax.dynamic_index_in_dim(ranks, seq_rank, 1, keepdims=False)
    slots = own_owner * capacity + own_rank
    own_perm = lax.dynamic_slice_in_dim(segment_partner_chart, seq_rank * blocks_dev, blocks_dev, 1)
    columns = jnp.arange(all_blocks, dtype=jnp.int32)
    hits = columns[None, None, :] == own_perm.T[:, :, None]
    bias = jnp.sum(jnp.where(hits, exponent_joint_density[:, None, :], 0.0), axis=-1)
    query_five = request_embeddings.reshape(blocks_dev, BLOCK, groups_dev, GROUP_HEADS, HEAD_DIM)
    kv_six = attended_content_pile.reshape(2, blocks_dev, BLOCK, groups_dev, GROUP_HEADS, HEAD_DIM)
    kv_blocks = attended_content_pile.reshape(2, blocks_dev, BLOCK, groups_dev, group_width)
    local_part = part_stats(query_five, kv_six[0], kv_six[1])
    outgoing_kv = take_blocks(kv_blocks, send_index, send_valid).reshape(
        2, seq_count, capacity, BLOCK, groups_dev, group_width
    )
    incoming = lax.all_to_all(outgoing_kv, "seq", split_axis=1, concat_axis=1, tiled=True)
    incoming = incoming.reshape(2, seq_count * capacity, BLOCK, groups_dev, group_width)
    matched_kv = jnp.stack([jnp.take(incoming[:, :, :, 0], slots[0], axis=1)], axis=3)
    matched_kv = matched_kv.reshape(2, blocks_dev, BLOCK, groups_dev, GROUP_HEADS, HEAD_DIM)
    matched_part = part_stats(query_five, matched_kv[0], matched_kv[1])
    mixed, entropy_block = combine_parts(local_part, matched_part, bias)
    attended = mixed.reshape(tokens_dev, local_width).astype(jnp.bfloat16)
    entropy = entropy_block.reshape(blocks_dev, local_heads).T
    return (attended, entropy)


def solution(mesh):
    in_specs = (P("seq", "heads"), P(None, "seq", "heads"), P(), P("heads", None))
    out_specs = (P("seq", "heads"), P("heads", "seq"))
    return jax.shard_map(
        on_device, mesh=mesh, in_specs=in_specs, out_specs=out_specs, check_vma=False
    )
```

profile of v0, /device:TPU:1, one launch (start us, length us, event | category | flops | bytes accessed | tf_op | source)
XLA Modules:
  0.0 613.8 jit_solution(780112342657812074)
XLA Ops:
  13.9 7.1 %gather_fusion = bf16[32,2,128,512]{3,2,1,0:T(8,128)(2,1)} fusion(bf16[2,16,128,512]{3,2,1,0:T(8,128)(2,1)} %bitcast.273, s32[1024]{0:T(1024)S(1)} %pad_clamp_fusion.1), kind=kCustom, calls=%fused_computation | custom fusion | bytes 16777344 | tf_op jit(solution)/shard_map/jit(_take)/gather | solution.py:87
  21.1 7.6 %fusion.1 = bf16[2,32,1,128,1,512]{5,3,0,4,2,1:T(8,128)(2,1)} fusion(bf16[32,2,128,512]{3,2,1,0:T(8,128)(2,1)} %gather_fusion, pred[32]{0:T(512)(128)(4,1)S(1)} %compare_and_fusion, pred[32]{0:T(512)(128)(4,1)S(1)} %get-tuple-element.1195), kind=kLoop, calls=%fused_computation.28 | loop fusion | flops 8388608 | bytes 16777280 | tf_op jit(solution)/shard_map/jit(_where)/select_n | solution.py:89
  28.6 8.6 %all-to-all-start = ((bf16[2,32,1,128,1,512]{5,3,0,4,2,1:T(8,128)(2,1)}), bf16[2,32,1,128,1,512]{5,3,0,4,2,1:T(8,128)(2,1)}, u32[]{:S(2)}, u32[]{:S(2)}) async-start(bf16[2,32,1,128,1,512]{5,3,0,4,2,1:T(8,128)(2,1)} %fusion.1), calls=%async_computation | async-start | bytes 16777216 | tf_op jit(solution)/shard_map/all_to_all | solution.py:146
  57.1 45.8 %all-gather.34.cloned.1.call-done = f32[512,512]{1,0:T(8,128)} async-done(((f32[16,512]{1,0:T(8,128)}), f32[512,512]{1,0:T(8,128)}) %all-gather.34.cloned.1.call-update) | async-done | bytes 1048592 | tf_op jit(solution)/shard_map/all_gather | solution.py:114
  105.1 24.0 %psum.7 = f32[16,512]{1,0:T(8,128)S(1)} all-reduce(f32[16,512]{1,0:T(8,128)S(1)} %convolution_multiply_fusion), channel_id=1, replica_groups=mesh['heads'=8,'seq'=32] {'heads'}, use_global_device_ids=true, to_apply=%region_7.0 | all-reduce | flops 8192 | bytes 65536 | tf_op jit(solution)/shard_map/psum | solution.py:117
  132.2 50.3 %all-gather.17 = f32[32,1,512]{2,1,0:T(1,128)S(1)} all-gather(f32[1,1,512]{2,1,0:T(1,128)S(1)} %bitcast.337), channel_id=3, replica_groups=mesh['heads'=8,'seq'=32] {'seq'}, dimensions={0}, use_global_device_ids=true | all-gather | bytes 67584 | tf_op jit(solution)/shard_map/all_gather | solution.py:16
  182.5 22.7 %all-gather.16 = f32[32,1,512]{2,1,0:T(1,128)S(1)} all-gather(f32[1,1,512]{2,1,0:T(1,128)S(1)} %bitcast.328), channel_id=2, replica_groups=mesh['heads'=8,'seq'=32] {'seq'}, dimensions={0}, use_global_device_ids=true | all-gather | bytes 67584 | tf_op jit(solution)/shard_map/all_gather | solution.py:16
  210.1 22.7 %all-gather.19 = f32[32,1,512]{2,1,0:T(1,128)S(1)} all-gather(f32[1,1,512]{2,1,0:T(1,128)S(1)} %bitcast.338), channel_id=5, replica_groups=mesh['heads'=8,'seq'=32] {'seq'}, dimensions={0}, use_global_device_ids=true | all-gather | bytes 67584 | tf_op jit(solution)/shard_map/all_gather | solution.py:16
  232.8 22.9 %all-gather.18 = f32[32,1,512]{2,1,0:T(1,128)S(1)} all-gather(f32[1,1,512]{2,1,0:T(1,128)S(1)} %bitcast.329), channel_id=4, replica_groups=mesh['heads'=8,'seq'=32] {'seq'}, dimensions={0}, use_global_device_ids=true | all-gather | bytes 67584 | tf_op jit(solution)/shard_map/all_gather | solution.py:16
  260.6 22.7 %all-gather.21 = f32[32,1,512]{2,1,0:T(1,128)S(1)} all-gather(f32[1,1,512]{2,1,0:T(1,128)S(1)} %bitcast.339), channel_id=7, replica_groups=mesh['heads'=8,'seq'=32] {'seq'}, dimensions={0}, use_global_device_ids=true | all-gather | bytes 67584 | tf_op jit(solution)/shard_map/all_gather | solution.py:16
  283.4 22.7 %all-gather.20 = f32[32,1,512]{2,1,0:T(1,128)S(1)} all-gather(f32[1,1,512]{2,1,0:T(1,128)S(1)} %bitcast.330), channel_id=6, replica_groups=mesh['heads'=8,'seq'=32] {'seq'}, dimensions={0}, use_global_device_ids=true | all-gather | bytes 67584 | tf_op jit(solution)/shard_map/all_gather | solution.py:16
  311.2 22.7 %all-gather.23 = f32[32,1,512]{2,1,0:T(1,128)S(1)} all-gather(f32[1,1,512]{2,1,0:T(1,128)S(1)} %bitcast.340), channel_id=9, replica_groups=mesh['heads'=8,'seq'=32] {'seq'}, dimensions={0}, use_global_device_ids=true | all-gather | bytes 67584 | tf_op jit(solution)/shard_map/all_gather | solution.py:16
  333.9 22.7 %all-gather.22 = f32[32,1,512]{2,1,0:T(1,128)S(1)} all-gather(f32[1,1,512]{2,1,0:T(1,128)S(1)} %bitcast.331), channel_id=8, replica_groups=mesh['heads'=8,'seq'=32] {'seq'}, dimensions={0}, use_global_device_ids=true | all-gather | bytes 67584 | tf_op jit(solution)/shard_map/all_gather | solution.py:16
  361.8 22.7 %all-gather.25 = f32[32,1,512]{2,1,0:T(1,128)S(1)} all-gather(f32[1,1,512]{2,1,0:T(1,128)S(1)} %bitcast.341), channel_id=11, replica_groups=mesh['heads'=8,'seq'=32] {'seq'}, dimensions={0}, use_global_device_ids=true | all-gather | bytes 67584 | tf_op jit(solution)/shard_map/all_gather | solution.py:16
  384.5 22.7 %all-gather.24 = f32[32,1,512]{2,1,0:T(1,128)S(1)} all-gather(f32[1,1,512]{2,1,0:T(1,128)S(1)} %bitcast.332), channel_id=10, replica_groups=mesh['heads'=8,'seq'=32] {'seq'}, dimensions={0}, use_global_device_ids=true | all-gather | bytes 67584 | tf_op jit(solution)/shard_map/all_gather | solution.py:16
  412.0 22.7 %all-gather.27 = f32[32,1,512]{2,1,0:T(1,128)S(1)} all-gather(f32[1,1,512]{2,1,0:T(1,128)S(1)} %bitcast.342), channel_id=13, replica_groups=mesh['heads'=8,'seq'=32] {'seq'}, dimensions={0}, use_global_device_ids=true | all-gather | bytes 67584 | tf_op jit(solution)/shard_map/all_gather | solution.py:16
  434.8 22.7 %all-gather.26 = f32[32,1,512]{2,1,0:T(1,128)S(1)} all-gather(f32[1,1,512]{2,1,0:T(1,128)S(1)} %bitcast.333), channel_id=12, replica_groups=mesh['heads'=8,'seq'=32] {'seq'}, dimensions={0}, use_global_device_ids=true | all-gather | bytes 67584 | tf_op jit(solution)/shard_map/all_gather | solution.py:16
  462.3 22.7 %all-gather.29 = f32[32,1,512]{2,1,0:T(1,128)S(1)} all-gather(f32[1,1,512]{2,1,0:T(1,128)S(1)} %bitcast.343), channel_id=15, replica_groups=mesh['heads'=8,'seq'=32] {'seq'}, dimensions={0}, use_global_device_ids=true | all-gather | bytes 67584 | tf_op jit(solution)/shard_map/all_gather | solution.py:16
  485.1 22.7 %all-gather.28 = f32[32,1,512]{2,1,0:T(1,128)S(1)} all-gather(f32[1,1,512]{2,1,0:T(1,128)S(1)} %bitcast.334), channel_id=14, replica_groups=mesh['heads'=8,'seq'=32] {'seq'}, dimensions={0}, use_global_device_ids=true | all-gather | bytes 67584 | tf_op jit(solution)/shard_map/all_gather | solution.py:16
  512.8 22.7 %all-gather.31 = f32[32,1,512]{2,1,0:T(1,128)S(1)} all-gather(f32[1,1,512]{2,1,0:T(1,128)S(1)} %bitcast.344), channel_id=17, replica_groups=mesh['heads'=8,'seq'=32] {'seq'}, dimensions={0}, use_global_device_ids=true | all-gather | bytes 67584 | tf_op jit(solution)/shard_map/all_gather | solution.py:16
  535.5 22.9 %all-gather.30 = f32[32,1,512]{2,1,0:T(1,128)S(1)} all-gather(f32[1,1,512]{2,1,0:T(1,128)S(1)} %bitcast.335), channel_id=16, replica_groups=mesh['heads'=8,'seq'=32] {'seq'}, dimensions={0}, use_global_device_ids=true | all-gather | bytes 67584 | tf_op jit(solution)/shard_map/all_gather | solution.py:16
  561.1 7.6 %copy.158 = bf16[2,32,1,128,1,512]{5,3,1,0,4,2:T(8,128)(2,1)} copy(bf16[2,32,1,128,1,512]{5,3,0,4,2,1:T(8,128)(2,1)} %all-to-all-done) | data formatting | bytes 16777216 | tf_op jit(solution)/shard_map/all_to_all | solution.py:146
  568.7 6.1 gather_fusion.1
  595.8 7.7 %fusion.3 = bf16[16,128,1,4,128]{4,1,3,0,2:T(8,128)(2,1)S(1)} fusion(f32[16,4,128,128]{3,2,1,0:T(8,128)} %fusion.10, bf16[16,128,4,128]{1,3,2,0:T(8,128)(2,1)} %bitcast.277, f32[16,4,128,128]{2,3,1,0:T(8,128)} %copy-done, f32[16,128,4]{1,2,0:T(4,128)S(1)} %get-tuple-element.1218, f32[16,128,4]{1,2,0:T(4,128)S(1)} %get-tuple-element.1217, ...), kind=kOutput, calls=%fused_computation.32 | convolution fusion | flops 275775488 | bytes 12681216 | tf_op jit(solution)/shard_map/mghqk,mkgha->mqgha/dot_general | solution.py:59
  (652 shorter events, 101.4 us)
Async XLA Ops:
  7.2 5.4 copy-start.4
  7.2 95.8 %all-gather.34.cloned.1.call-start = ((), (), s32[]{:S(2)}) async-start(), calls=%async_computation.1 | async-start | bytes 1081344 | tf_op jit(solution)/shard_map/all_gather | solution.py:114
  28.6 532.5 %all-to-all-start = ((bf16[2,32,1,128,1,512]{5,3,0,4,2,1:T(8,128)(2,1)}), bf16[2,32,1,128,1,512]{5,3,0,4,2,1:T(8,128)(2,1)}, u32[]{:S(2)}, u32[]{:S(2)}) async-start(bf16[2,32,1,128,1,512]{5,3,0,4,2,1:T(8,128)(2,1)} %fusion.1), calls=%async_computation | async-start | bytes 16777216 | tf_op jit(solution)/shard_map/all_to_all | solution.py:146
  39.6 6.6 %copy-start.3 = (f32[8]{0:T(128)S(1)}, f32[8]{0:T(128)}, u32[]{:S(2)}) copy-start(f32[8]{0:T(128)} %param.22) | copy-start | bytes 100
  52.1 2.0 copy-start.1
  586.8 2.1 copy-start
  586.8 6.6 %copy-start.2 = (bf16[1,16,128,512]{3,2,0,1:T(8,128)(2,1)S(1)}, bf16[1,16,128,512]{3,2,0,1:T(8,128)(2,1)}, u32[]{:S(2)}) copy-start(bf16[1,16,128,512]{3,2,0,1:T(8,128)(2,1)} %get-tuple-element.1214) | copy-start | bytes 6291460
Sparse Core Ops, SparseCore 0:
  12.1 90.8 all-gather.33
where the time goes:
time: 615 us; the launch traced here: 614 us
  blocking collectives  415 us (67%)
  local copies, waits for them, and re-layouts  53.4 us (9%)
  other arithmetic  50.4 us (8%)
  waiting for transfers between devices  45.9 us (7%)
  matrix products  19.1 us (3%)
  between operations  14.6 us (2%)
  starting transfers between devices  8.67 us (1%)
  loops' own time  6.58 us (1%)
    all_gather x16, blocking collectives, merged(): everything = jax.tree.map(lambda part: lax.all_gather(part, axis), array)  391 us
    all_gather x1, waiting for transfers between devices, on_device(): lax.all_gather(key_sums, 'seq', axis=0, tiled=True)  45.8 us
    psum x1, blocking collectives, on_device(): request_potentials = lax.psum(incomplete_price * price_multiplier, 'heads')  24 us
  transfers between devices with their start and end apart: 2, of which 1 were waited for; matrix products, arithmetic and copies ran while one was open for 12% of the time, Pallas kernels for 0%

commit v1 on v0

v1 whole, which is shorter than its diff:
```python
import math

import jax
import jax.numpy as jnp
from jax import lax
from jax.experimental import pallas as pl
from jax.experimental.pallas import tpu as pltpu
from jax.sharding import PartitionSpec as P

HEADS = 32
HEAD_DIM = 128
BLOCK = 128
GROUP_HEADS = 4
REFIT_REPEATS = 8
WIDTH = GROUP_HEADS * HEAD_DIM
BLOCKS_DEV = 16
N_SEQ = 32
N_HEADS = 8
ALL_BLOCKS = BLOCKS_DEV * N_SEQ
MESH = pl.DeviceIdType.MESH
F32 = jnp.float32
PRICE = 1.0 / (BLOCK * math.sqrt(HEAD_DIM * HEADS))
SCALE = HEAD_DIM ** (-0.5)
WANTED, QUERY, COLUMN, OWNER = range(4)


def split_slot(t):
    return t // 8, (t // 2) % 4, t % 2


def kernel(
    route, soft, q_ref, kv_ref, att_ref, ent_ref,
    pack_k, pack_v, mid_k, mid_v, fin_k, fin_v, out_slot, ent_slot,
    q_sum, k_sum, part, part_in, cost, row_pot, col_pot, mine,
    sum_send, sum_recv, red_send, red_recv, tile_send, tile_recv,
    first_k_send, first_v_send, mid_k_recv, mid_v_recv,
    second_k_send, second_v_send, fin_k_recv, fin_v_recv,
):
    seq = lax.axis_index("seq")
    z = lax.axis_index("heads")
    x, y, c = seq // 8, (seq // 2) % 4, seq % 2
    yc = seq % 8

    def place(dx, dy, dc):
        return lax.rem(x + dx, 4) * 8 + lax.rem(y + dy, 4) * 2 + lax.rem(c + dc, 2)

    def device(dx, dy, dc):
        return (z, place(dx, dy, dc))

    def floor(dz):
        return (lax.rem(z + dz, N_HEADS), seq)

    def remote(src, dst, send, recv, to):
        return pltpu.make_async_remote_copy(
            src_ref=src, dst_ref=dst, send_sem=send, recv_sem=recv, device_id=to, device_id_type=MESH
        )

    barrier = pltpu.get_barrier_semaphore()
    peers = [device(d, 0, e) for d in (1, 2, 3) for e in (0, 1)]
    peers += [device(0, d, e) for d in (1, 2, 3) for e in (0, 1)]
    peers += [device(0, 0, 1)] + [floor(d) for d in range(1, N_HEADS)]
    for peer in peers:
        pl.semaphore_signal(barrier, inc=1, device_id=peer, device_id_type=MESH)

    tokens = BLOCKS_DEV * BLOCK
    owner = lax.broadcasted_iota(jnp.int32, (BLOCKS_DEV, tokens), 1) // BLOCK
    ones = jnp.where(owner == lax.broadcasted_iota(jnp.int32, (BLOCKS_DEV, tokens), 0), 1.0, 0.0).astype(jnp.bfloat16)
    q_rows = pl.ds(pl.multiple_of(x * BLOCKS_DEV, BLOCKS_DEV), BLOCKS_DEV)
    k_rows = pl.ds(pl.multiple_of(yc * BLOCKS_DEV, BLOCKS_DEV), BLOCKS_DEV)
    q_sum[q_rows, :] = jnp.dot(ones, q_ref[...].reshape(tokens, WIDTH), preferred_element_type=F32)
    k_sum[k_rows, :] = jnp.dot(ones, kv_ref[0].reshape(tokens, WIDTH), preferred_element_type=F32)

    pl.semaphore_wait(barrier, len(peers))

    sums = []
    for d in (1, 2, 3):
        sums.append(remote(q_sum.at[q_rows], q_sum.at[q_rows], sum_send.at[d], sum_recv.at[d], device(d, 0, 0)))
    for r in range(1, 8):
        sums.append(
            remote(k_sum.at[k_rows], k_sum.at[k_rows], sum_send.at[3 + r], sum_recv.at[3 + r], device(0, r // 2, r % 2))
        )
    for copy in sums:
        copy.start()

    def first_k(t, final):
        dst, recv = (fin_k, fin_k_recv) if final else (mid_k, mid_k_recv)
        return remote(pack_k.at[t], dst.at[t], first_k_send.at[t], recv.at[t], device(t // 8, 0, 0))

    def first_v(t, final):
        dst, recv = (fin_v, fin_v_recv) if final else (mid_v, mid_v_recv)
        return remote(pack_v.at[t], dst.at[t], first_v_send.at[t], recv.at[t], device(0, (t // 2) % 4, 0))

    def second_k(t, direct):
        src = pack_k if direct else mid_k
        _, dy, dc = split_slot(t)
        return remote(src.at[t], fin_k.at[t], second_k_send.at[t], fin_k_recv.at[t], device(0, dy, dc))

    def second_v(t, direct):
        src = pack_v if direct else mid_v
        dx, _, dc = split_slot(t)
        return remote(src.at[t], fin_v.at[t], second_v_send.at[t], fin_v_recv.at[t], device(dx, 0, dc))

    def rest_k(d):
        return lambda u: d * 8 + 1 + u

    def rest_v(d):
        def slot(u):
            w = u + 1
            return (w // 2) * 8 + d * 2 + w % 2

        return slot

    def each(count, action):
        def step(u, carry):
            action(u)
            return carry

        lax.fori_loop(0, count, step, 0)

    def fill_k(t, into):
        into[t] = kv_ref[0, route[WANTED, place(*split_slot(t))]]

    def fill_v(t, into):
        into[t] = kv_ref[1, route[WANTED, place(*split_slot(t))]]

    for d in (2, 1, 3):
        def start_k(u, d=d):
            t = rest_k(d)(u)
            fill_k(t, pack_k)
            first_k(t, False).start()

        def start_v(u, d=d):
            t = rest_v(d)(u)
            fill_v(t, pack_v)
            first_v(t, False).start()

        each(7, start_k)
        each(7, start_v)
    for d in (2, 1, 3):
        fill_k(d * 8, pack_k)
        first_k(d * 8, True).start()
        fill_v(d * 2, pack_v)
        first_v(d * 2, True).start()

    fill_k(0, fin_k)
    fill_v(0, fin_v)

    def start_near_k(u):
        t = rest_k(0)(u)
        fill_k(t, pack_k)
        second_k(t, True).start()

    def start_near_v(u):
        t = rest_v(0)(u)
        fill_v(t, pack_v)
        second_v(t, True).start()

    for copy in sums:
        copy.wait()
    shares = lax.dot_general(
        q_sum[...], k_sum[...], (((1,), (1,)), ((), ())), precision=lax.Precision.HIGHEST, preferred_element_type=F32
    )
    part[...] = (shares * PRICE).reshape(N_HEADS, 8, 128)
    reduces = []
    for d in range(1, N_HEADS):
        to = lax.rem(z + d, N_HEADS)
        reduces.append(remote(part.at[to], part_in.at[z], red_send.at[d], red_recv.at[d], floor(d)))
    for copy in reduces:
        copy.start()
    part_in[z] = part[z]
    for copy in reduces:
        copy.wait()
    cost[z, yc, x] = jnp.sum(part_in[...], axis=0)
    tiles = []
    for d in (1, 2, 3):
        tile = cost.at[z, yc, x]
        tiles.append(remote(tile, tile, tile_send.at[d], tile_recv.at[d], device(d, 0, 0)))
    for copy in tiles:
        copy.start()
    for copy in tiles:
        copy.wait()
    tiles = []
    for r in range(1, 8):
        strip = cost.at[z, yc]
        tiles.append(remote(strip, strip, tile_send.at[3 + r], tile_recv.at[3 + r], device(0, r // 2, r % 2)))
    for copy in tiles:
        copy.start()
    for copy in tiles:
        copy.wait()
    tiles = []
    for d in range(1, N_HEADS):
        layer = cost.at[z]
        tiles.append(remote(layer, layer, tile_send.at[10 + d], tile_recv.at[10 + d], floor(d)))
    for copy in tiles:
        copy.start()

    for d in (2, 1, 3):
        def pass_k(u, d=d):
            t = rest_k(d)(u)
            first_k(t, False).wait_recv()
            second_k(t, False).start()

        def pass_v(u, d=d):
            t = rest_v(d)(u)
            first_v(t, False).wait_recv()
            second_v(t, False).start()

        each(7, pass_k)
        each(7, pass_v)
    each(7, start_near_k)
    each(7, start_near_v)

    for copy in tiles:
        copy.wait()

    col_pot[...] = jnp.zeros_like(col_pot)

    def refit(repeat, carry):
        inverse = 1.0 / soft[repeat]

        def rows(k, carry):
            scaled = cost[k] * inverse + col_pot[...][None]
            top = jnp.max(jnp.max(scaled, axis=1), axis=-1, keepdims=True)
            total = jnp.sum(jnp.sum(jnp.exp(scaled - top[:, None]), axis=1), axis=-1, keepdims=True)
            row_pot[k] = jnp.broadcast_to(-(top + jnp.log(total)), (8, 8, 128))
            return carry

        lax.fori_loop(0, N_HEADS, rows, 0)

        def tops(k, top):
            scaled = cost[k] * inverse + row_pot[k][:, None]
            return jnp.maximum(top, jnp.max(scaled, axis=0))

        top = lax.fori_loop(0, N_HEADS, tops, jnp.full((4, 8, 128), -jnp.inf, F32))
        top = jnp.broadcast_to(jnp.max(top, axis=1, keepdims=True), (4, 8, 128))

        def totals(k, total):
            scaled = cost[k] * inverse + row_pot[k][:, None]
            return total + jnp.sum(jnp.exp(scaled - top[None]), axis=0)

        total = lax.fori_loop(0, N_HEADS, totals, jnp.zeros((4, 8, 128), F32))
        total = jnp.broadcast_to(jnp.sum(total, axis=1, keepdims=True), (4, 8, 128))
        col_pot[...] = -(top + jnp.log(total))
        return carry

    lax.fori_loop(0, REFIT_REPEATS, refit, 0)
    inverse = 1.0 / soft[REFIT_REPEATS - 1]
    for half in range(2):
        k = x * 2 + half
        coupling = cost[k, yc] * inverse + row_pot[k, yc][None] + col_pot[...] + math.log(ALL_BLOCKS)
        for column in range(4):
            mine[half * 8 : half * 8 + 8, column * 128 : column * 128 + 128] = coupling[column]

    columns = lax.broadcasted_iota(jnp.int32, (BLOCKS_DEV, ALL_BLOCKS), 1)
    queries = lax.broadcasted_iota(jnp.int32, (BLOCKS_DEV, ALL_BLOCKS), 0)

    def attend(t):
        dx, dy, dc = split_slot(t)
        source = place(4 - dx, 4 - dy, dc)
        index, column = route[QUERY, source], route[COLUMN, source]
        entry = jnp.logical_and(columns == column, queries == index)
        bias = jnp.sum(jnp.sum(jnp.where(entry, mine[...], 0.0), axis=0, keepdims=True), axis=1, keepdims=True)
        for h in range(GROUP_HEADS):
            lanes = slice(h * HEAD_DIM, (h + 1) * HEAD_DIM)
            q = q_ref[index, :, lanes]
            turned = (((1,), (1,)), ((), ()))
            near = lax.dot_general(kv_ref[0, index, :, lanes], q, turned, preferred_element_type=F32) * SCALE
            far = lax.dot_general(fin_k[t, :, lanes], q, turned, preferred_element_type=F32) * SCALE + bias
            joint = jnp.maximum(jnp.max(near, axis=0, keepdims=True), jnp.max(far, axis=0, keepdims=True))
            near_expo, far_expo = jnp.exp(near - joint), jnp.exp(far - joint)
            total = jnp.sum(near_expo, axis=0, keepdims=True) + jnp.sum(far_expo, axis=0, keepdims=True)
            moment = jnp.sum(near_expo * near + far_expo * far, axis=0, keepdims=True)
            share = 1.0 / total
            down = (((0,), (0,)), ((), ()))
            mixed = lax.dot_general(
                (near_expo * share).astype(jnp.bfloat16), kv_ref[1, index, :, lanes], down, preferred_element_type=F32
            ) + lax.dot_general(
                (far_expo * share).astype(jnp.bfloat16), fin_v[t, :, lanes], down, preferred_element_type=F32
            )
            out_slot[source, :, lanes] = mixed.astype(jnp.bfloat16)
            ent_slot[source, h : h + 1, :] = jnp.log(total) + joint - moment * share

    attend(0)

    def arrived(t):
        second_k(t, True).wait_recv()
        second_v(t, True).wait_recv()
        attend(t)

    each(N_SEQ - 1, lambda u: arrived(u + 1))

    lane = lax.broadcasted_iota(jnp.int32, (GROUP_HEADS, 128), 1)
    entropy = jnp.zeros((GROUP_HEADS, 128), F32)
    for i in range(BLOCKS_DEV):
        source = route[OWNER, i]
        att_ref[i] = out_slot[source]
        mean = jnp.sum(ent_slot[source], axis=1, keepdims=True) * (1.0 / BLOCK)
        entropy = jnp.where(lane == i, mean, entropy)
    ent_ref[...] = entropy[:, :BLOCKS_DEV]

    for d in (1, 2, 3):
        each(8, lambda u, d=d: first_k(d * 8 + u, False).wait_send())
        each(8, lambda u, d=d: first_v((u // 2) * 8 + d * 2 + u % 2, False).wait_send())
    for d in range(4):
        each(7, lambda u, d=d: second_k(rest_k(d)(u), True).wait_send())
        each(7, lambda u, d=d: second_v(rest_v(d)(u), True).wait_send())


def routes(chart):
    seq = lax.axis_index("seq")
    table = chart.reshape(N_SEQ, BLOCKS_DEV)
    wanted = jnp.sum(jnp.where(table // BLOCKS_DEV == seq, table % BLOCKS_DEV, 0), axis=1)
    own = lax.dynamic_index_in_dim(table, seq, 0, keepdims=False)
    owner = own // BLOCKS_DEV
    hit = jnp.arange(N_SEQ, dtype=jnp.int32)[:, None] == owner[None, :]
    query = jnp.sum(jnp.where(hit, jnp.arange(BLOCKS_DEV, dtype=jnp.int32)[None, :], 0), axis=1)
    column = jnp.sum(jnp.where(hit, own[None, :], 0), axis=1)
    return jnp.stack([wanted, query, column, jnp.concatenate([owner, owner])])


def on_device(queries, pile, softness, chart):
    slots = pltpu.VMEM((N_SEQ, BLOCK, WIDTH), jnp.bfloat16)
    dma = pltpu.SemaphoreType.DMA
    smem = pl.BlockSpec(memory_space=pltpu.SMEM)
    vmem = pl.BlockSpec(memory_space=pltpu.VMEM)
    attended, entropy = pl.pallas_call(
        kernel,
        out_shape=(
            jax.ShapeDtypeStruct((BLOCKS_DEV, BLOCK, WIDTH), jnp.bfloat16),
            jax.ShapeDtypeStruct((GROUP_HEADS, BLOCKS_DEV), F32),
        ),
        in_specs=[smem, smem, vmem, vmem],
        out_specs=(vmem, vmem),
        scratch_shapes=[
            slots, slots, slots, slots, slots, slots, slots,
            pltpu.VMEM((N_SEQ, GROUP_HEADS, 128), F32),
            pltpu.VMEM((64, WIDTH), F32),
            pltpu.VMEM((128, WIDTH), F32),
            pltpu.VMEM((N_HEADS, 8, 128), F32),
            pltpu.VMEM((N_HEADS, 8, 128), F32),
            pltpu.VMEM((N_HEADS, 8, 4, 8, 128), F32),
            pltpu.VMEM((N_HEADS, 8, 8, 128), F32),
            pltpu.VMEM((4, 8, 128), F32),
            pltpu.VMEM((BLOCKS_DEV, ALL_BLOCKS), F32),
            dma((11,)), dma((11,)), dma((8,)), dma((8,)), dma((18,)), dma((18,)),
            dma((N_SEQ,)), dma((N_SEQ,)), dma((N_SEQ,)), dma((N_SEQ,)),
            dma((N_SEQ,)), dma((N_SEQ,)), dma((N_SEQ,)), dma((N_SEQ,)),
        ],
        compiler_params=pltpu.CompilerParams(
            collective_id=0, has_side_effects=True, vmem_limit_bytes=60 * 1024 * 1024
        ),
        name="sparse_attention",
    )(
        routes(chart), softness, queries.reshape(BLOCKS_DEV, BLOCK, WIDTH), pile.reshape(2, BLOCKS_DEV, BLOCK, WIDTH)
    )
    return attended.reshape(queries.shape), entropy


def solution(mesh):
    in_specs = (P("seq", "heads"), P(None, "seq", "heads"), P(), P("heads", None))
    out_specs = (P("seq", "heads"), P("heads", "seq"))
    return jax.shard_map(
        on_device, mesh=mesh, in_specs=in_specs, out_specs=out_specs, check_vma=False
    )
```

time: 615 us -> 163 us (0.27)
  blocking collectives: 415 us -> 0 us
  Pallas kernels: 0 us -> 156 us
  local copies, waits for them, and re-layouts: 53.4 us -> 4.22 us
  other arithmetic: 50.4 us -> 2.29 us
  waiting for transfers between devices: 45.9 us -> 0 us
  matrix products: 19.1 us -> 0 us
  between operations: 14.6 us -> 0.67 us
  starting transfers between devices: 8.67 us -> 0 us
  loops' own time: 6.58 us -> 0 us
    all_gather x16 -> x0, blocking collectives: 391 us -> none  [merged(): everything = jax.tree.map(lambda part: lax.all_gather(part, axis), array)]
    pallas_call x0 -> x1, Pallas kernels: none -> 156 us  [on_device(): pl.pallas_call(kernel, out_shape=(jax.ShapeDtypeStruct((BLOCKS_DEV, BLOCK...]
    all_gather x1 -> x0, waiting for transfers between devices: 45.8 us -> none  [on_device(): lax.all_gather(key_sums, 'seq', axis=0, tiled=True)]
    psum x1 -> x0, blocking collectives: 24 us -> none  [on_device(): request_potentials = lax.psum(incomplete_price * price_multiplier, 'heads')]
    reduce_sum x24 -> x2, other arithmetic: 22 us -> 0.24 us  [the longest x1 0.13 us: routes(): jnp.sum(jnp.where(table // BLOCKS_DEV == seq, table % BLOCKS_DEV, 0), axi...]
    dot_general x5 -> x0, matrix products: 19.1 us -> none  [the longest x2 10.8 us: part_stats(): jnp.einsum('mghqk,mkgha->mqgha', weights, values_five, preferred_element_...]
    slice x21 -> x0, local copies, waits for them, and re-layouts: 13.3 us -> none  [the longest x3 8.77 us: on_device(): matched_part = part_stats(query_five, matched_kv[0], matched_kv[1])]
    gather x2 -> x0, local copies, waits for them, and re-layouts: 13.2 us -> none  [the longest x1 7.12 us: take_blocks(): picked = jnp.take(kv_blocks[:, :, :, 0], send_index[0].reshape(-1), axis=1)]
  transfers between devices with their start and end apart: 2 -> 0, of which waited for: 1 -> 0; matrix products, arithmetic and copies ran while one was open for 12% -> 0% of each run, Pallas kernels for 0% -> 0%
where the time goes in v1:
time: 163 us
  Pallas kernels  156 us (96%)
  local copies, waits for them, and re-layouts  4.22 us (3%)
  other arithmetic  2.29 us (1%)
    pallas_call x1, Pallas kernels, on_device(): pl.pallas_call(kernel, out_shape=(jax.ShapeDtypeStruct((BLOCKS_DEV, BLOCK...  156 us
    unnamed x5, local copies, waits for them, and re-layouts  4.14 us

profile of v1, /device:TPU:1, one launch (start us, length us, event | category | flops | bytes accessed | tf_op | source)
XLA Modules:
  0.0 162.8 jit_solution(2258692355520681971)
XLA Ops:
  0.6 0.5 broadcast.88
  1.1 1.3 reduce.3
  2.5 0.1 reshape.16
  2.6 0.1 fusion.2
  2.7 0.1 add_bitcast_fusion
  2.8 0.1 select_reduce_fusion.1
  2.9 0.6 pad_add_fusion.route
  3.5 155.6 %sparse_attention.1 = (bf16[16,128,512]{2,1,0:T(8,128)(2,1)}, f32[4,16]{1,0:T(4,128)}) custom-call(s32[4,32]{1,0:T(4,128)} %pad_add_fusion.route, f32[8]{0:T(128)} %soft.1, bf16[16,128,512]{2,1,0:T(8,128)(2,1)} %bitcast.14, bf16[2,16,128,512]{3,2,1,0:T(8,128)(2,1)} %bitcast.13), custom_call_target="tpu_custom_call" | custom-call | tf_op jit(solution)/shard_map/sparse_attention/pallas_call | solution.py:326
  159.2 0.0 copy-start
  159.2 3.0 %copy.8 = bf16[2048,512]{1,0:T(8,128)(2,1)} copy(bf16[2048,512]{1,0:T(8,128)(2,1)} %bitcast.15) | data formatting | bytes 4194304
  162.2 0.0 copy-done
  162.2 0.6 copy.9
  (2 shorter events, 0.0 us)
Async XLA Ops:
  159.2 3.1 %copy-start = (f32[4,16]{1,0:T(4,128)S(1)}, f32[4,16]{1,0:T(4,128)}, u32[]{:S(2)}) copy-start(f32[4,16]{1,0:T(4,128)} %get-tuple-element.13) | copy-start | bytes 772

commit v2 on v1

v2 whole, which is shorter than its diff:
```python
import math

import jax
import jax.numpy as jnp
from jax import lax
from jax.experimental import pallas as pl
from jax.experimental.pallas import tpu as pltpu
from jax.sharding import PartitionSpec as P

HEADS = 32
HEAD_DIM = 128
BLOCK = 128
GROUP_HEADS = 4
REFIT_REPEATS = 8
WIDTH = GROUP_HEADS * HEAD_DIM
BLOCKS_DEV = 16
N_SEQ = 32
N_HEADS = 8
ALL_BLOCKS = BLOCKS_DEV * N_SEQ
MESH = pl.DeviceIdType.MESH
F32 = jnp.float32
PRICE = 1.0 / (BLOCK * math.sqrt(HEAD_DIM * HEADS))
SCALE = HEAD_DIM ** (-0.5)
LOG2E = math.log2(math.e)
WANTED, QUERY, PARTNER, OWNER = range(4)


def split_slot(t):
    return t // 8, (t // 2) % 4, t % 2


def kernel(
    route, soft, q_hbm, kv_hbm, att_ref, ent_ref, q_ref, kv_ref, near_expo, near_stat,
    pack_k, pack_v, mid_k, mid_v, fin_k, fin_v, out_slot, ent_slot,
    q_sum, k_sum, part, part_in, cost, row_pot, col_pot, mine,
    load_sem, sum_send, sum_recv, red_send, red_recv, tile_send, tile_recv,
    first_k_send, first_v_send, mid_k_recv, mid_v_recv,
    second_k_send, second_v_send, fin_k_recv, fin_v_recv,
):
    seq = lax.axis_index("seq")
    z = lax.axis_index("heads")
    x, y, c = seq // 8, (seq // 2) % 4, seq % 2
    yc = seq % 8

    def place(dx, dy, dc):
        return lax.rem(x + dx, 4) * 8 + lax.rem(y + dy, 4) * 2 + lax.rem(c + dc, 2)

    def device(dx, dy, dc):
        return (z, place(dx, dy, dc))

    def floor(dz):
        return (lax.rem(z + dz, N_HEADS), seq)

    def remote(src, dst, send, recv, to):
        return pltpu.make_async_remote_copy(
            src_ref=src, dst_ref=dst, send_sem=send, recv_sem=recv, device_id=to, device_id_type=MESH
        )

    load_k = pltpu.make_async_copy(kv_hbm.at[0], kv_ref.at[0], load_sem.at[0])
    load_q = pltpu.make_async_copy(q_hbm, q_ref, load_sem.at[1])
    load_v = pltpu.make_async_copy(kv_hbm.at[1], kv_ref.at[1], load_sem.at[2])
    load_k.start()
    load_q.start()
    load_v.start()
    barrier = pltpu.get_barrier_semaphore()
    peers = [device(d, 0, e) for d in (1, 2, 3) for e in (0, 1)]
    peers += [device(0, d, e) for d in (1, 2, 3) for e in (0, 1)]
    peers += [device(0, 0, 1)] + [floor(d) for d in range(1, N_HEADS)]
    for peer in peers:
        pl.semaphore_signal(barrier, inc=1, device_id=peer, device_id_type=MESH)

    q_rows = pl.ds(pl.multiple_of(x * BLOCKS_DEV, BLOCKS_DEV), BLOCKS_DEV)
    k_rows = pl.ds(pl.multiple_of(yc * BLOCKS_DEV, BLOCKS_DEV), BLOCKS_DEV)
    load_k.wait()
    k_sum[k_rows, :] = jnp.sum(kv_ref[0].astype(F32), axis=1)
    load_q.wait()
    q_sum[q_rows, :] = jnp.sum(q_ref[...].astype(F32), axis=1)

    pl.semaphore_wait(barrier, len(peers))

    sums = []
    for d in (1, 2, 3):
        sums.append(remote(q_sum.at[q_rows], q_sum.at[q_rows], sum_send.at[d], sum_recv.at[d], device(d, 0, 0)))
    for r in range(1, 8):
        sums.append(
            remote(k_sum.at[k_rows], k_sum.at[k_rows], sum_send.at[3 + r], sum_recv.at[3 + r], device(0, r // 2, r % 2))
        )
    for copy in sums:
        copy.start()

    def first_k(t, final):
        dst, recv = (fin_k, fin_k_recv) if final else (mid_k, mid_k_recv)
        return remote(pack_k.at[t], dst.at[t], first_k_send.at[t], recv.at[t], device(t // 8, 0, 0))

    def first_v(t, final):
        dst, recv = (fin_v, fin_v_recv) if final else (mid_v, mid_v_recv)
        return remote(pack_v.at[t], dst.at[t], first_v_send.at[t], recv.at[t], device(0, (t // 2) % 4, 0))

    def second_k(t, direct):
        src = pack_k if direct else mid_k
        _, dy, dc = split_slot(t)
        return remote(src.at[t], fin_k.at[t], second_k_send.at[t], fin_k_recv.at[t], device(0, dy, dc))

    def second_v(t, direct):
        src = pack_v if direct else mid_v
        dx, _, dc = split_slot(t)
        return remote(src.at[t], fin_v.at[t], second_v_send.at[t], fin_v_recv.at[t], device(dx, 0, dc))

    def is_final_k(t):
        return t % 8 == 0

    def is_final_v(t):
        return t // 8 == 0 and t % 2 == 0

    def nth_slot(u):
        j = (u // 2) % 4
        return ((j + 1) % 4) * 8 + ((j + u // 8 + 1) % 4) * 2 + u % 2

    order = [nth_slot(u) for u in range(N_SEQ)]

    def fill_k(t, into):
        into[t] = kv_ref[0, route[WANTED, place(*split_slot(t))]]

    def fill_v(t, into):
        into[t] = kv_ref[1, route[WANTED, place(*split_slot(t))]]

    load_v.wait()
    for t in order:
        dx, dy, dc = split_slot(t)
        fill_k(t, pack_k if t else fin_k)
        if dx:
            first_k(t, is_final_k(t)).start()
        fill_v(t, pack_v if t else fin_v)
        if dy:
            first_v(t, is_final_v(t)).start()

    turned = (((1,), (1,)), ((), ()))

    heads = [slice(h * HEAD_DIM, (h + 1) * HEAD_DIM) for h in range(GROUP_HEADS)]

    def softmax_part(keys, queries):
        scores = [lax.dot_general(k, q, turned, preferred_element_type=F32) for k, q in zip(keys, queries)]
        tops = [jnp.max(score, axis=0, keepdims=True) for score in scores]
        expos = [jnp.exp2((score - top) * (SCALE * LOG2E)) for score, top in zip(scores, tops)]
        totals = [jnp.sum(expo, axis=0, keepdims=True) for expo in expos]
        moments = [jnp.sum(expo * score, axis=0, keepdims=True) for expo, score in zip(expos, scores)]
        stack = lambda rows: jnp.concatenate(rows, axis=0)
        return expos, stack(tops) * SCALE, stack(totals), stack(moments) * SCALE

    def near_part(i):
        expos, top, total, moment = softmax_part(
            [kv_ref[0, i, :, lanes] for lanes in heads], [q_ref[i, :, lanes] for lanes in heads]
        )
        for h in range(GROUP_HEADS):
            near_expo[i, h] = expos[h]
        near_stat[i, 0] = top
        near_stat[i, 1] = total
        near_stat[i, 2] = moment

    def near_parts(first):
        def step(u, carry):
            near_part(first + u)
            return carry

        lax.fori_loop(0, 4, step, 0)

    for copy in sums:
        copy.wait()
    shares = lax.dot_general(
        q_sum[...], k_sum[...], (((1,), (1,)), ((), ())), precision=lax.Precision.HIGHEST, preferred_element_type=F32
    )
    part[...] = (shares * PRICE).reshape(N_HEADS, 8, 128)
    reduces = []
    for d in range(1, N_HEADS):
        to = lax.rem(z + d, N_HEADS)
        reduces.append(remote(part.at[to], part_in.at[z], red_send.at[d], red_recv.at[d], floor(d)))
    for copy in reduces:
        copy.start()
    part_in[z] = part[z]
    near_parts(0)
    for copy in reduces:
        copy.wait()
    cost[z, yc, x] = jnp.sum(part_in[...], axis=0)
    tiles = []
    for d in (1, 2, 3):
        tile = cost.at[z, yc, x]
        tiles.append(remote(tile, tile, tile_send.at[d], tile_recv.at[d], device(d, 0, 0)))
    for copy in tiles:
        copy.start()
    near_parts(4)
    for copy in tiles:
        copy.wait()
    tiles = []
    for r in range(1, 8):
        strip = cost.at[z, yc]
        tiles.append(remote(strip, strip, tile_send.at[3 + r], tile_recv.at[3 + r], device(0, r // 2, r % 2)))
    for copy in tiles:
        copy.start()
    near_parts(8)
    for copy in tiles:
        copy.wait()
    tiles = []
    for d in range(1, N_HEADS):
        layer = cost.at[z]
        tiles.append(remote(layer, layer, tile_send.at[10 + d], tile_recv.at[10 + d], floor(d)))
    for copy in tiles:
        copy.start()

    near_parts(12)
    for t in order:
        dx, dy, dc = split_slot(t)
        if dx and not is_final_k(t):
            first_k(t, False).wait_recv()
        if not is_final_k(t):
            second_k(t, dx == 0).start()
        if dy and not is_final_v(t):
            first_v(t, False).wait_recv()
        if not is_final_v(t):
            second_v(t, dy == 0).start()

    for copy in tiles:
        copy.wait()

    col_pot[...] = jnp.zeros_like(col_pot)

    def refit(repeat, carry):
        inverse = LOG2E / soft[repeat]

        def rows(k, carry):
            scaled = cost[k] * inverse + col_pot[...][None]
            top = jnp.max(jnp.max(scaled, axis=1), axis=-1, keepdims=True)
            total = jnp.sum(jnp.sum(jnp.exp2(scaled - top[:, None]), axis=1), axis=-1, keepdims=True)
            row_pot[k] = jnp.broadcast_to(-(top + jnp.log2(total)), (8, 8, 128))
            return carry

        lax.fori_loop(0, N_HEADS, rows, 0, unroll=4)

        def tops(k, top):
            scaled = cost[k] * inverse + row_pot[k][:, None]
            return jnp.maximum(top, jnp.max(scaled, axis=0))

        top = lax.fori_loop(0, N_HEADS, tops, jnp.full((4, 8, 128), -jnp.inf, F32), unroll=2)
        top = jnp.broadcast_to(jnp.max(top, axis=1, keepdims=True), (4, 8, 128))

        def totals(k, total):
            scaled = cost[k] * inverse + row_pot[k][:, None]
            return total + jnp.sum(jnp.exp2(scaled - top[None]), axis=0)

        total = lax.fori_loop(0, N_HEADS, totals, jnp.zeros((4, 8, 128), F32), unroll=2)
        total = jnp.broadcast_to(jnp.sum(total, axis=1, keepdims=True), (4, 8, 128))
        col_pot[...] = -(top + jnp.log2(total))
        return carry

    lax.fori_loop(0, REFIT_REPEATS, refit, 0)
    inverse = LOG2E / soft[REFIT_REPEATS - 1]
    for half in range(2):
        k = x * 2 + half
        coupling = (cost[k, yc] * inverse + row_pot[k, yc][None] + col_pot[...]) * math.log(2.0) + math.log(ALL_BLOCKS)
        for column in range(4):
            mine[half * 8 : half * 8 + 8, column * 128 : column * 128 + 128] = coupling[column]

    queries = lax.broadcasted_iota(jnp.int32, (BLOCKS_DEV, 128), 0)
    partner = jnp.zeros((BLOCKS_DEV, 128), jnp.int32)
    for i in range(BLOCKS_DEV):
        partner = jnp.where(queries == i, route[PARTNER, i], partner)
    partner = jnp.concatenate([partner] * 4, axis=1)
    columns = lax.broadcasted_iota(jnp.int32, (BLOCKS_DEV, ALL_BLOCKS), 1)
    biases = jnp.sum(jnp.where(columns == partner, mine[...], 0.0), axis=1, keepdims=True)
    for i in range(BLOCKS_DEV):
        near_stat[i, 3] = jnp.broadcast_to(biases[i : i + 1], (GROUP_HEADS, 128))

    def attend(t):
        dx, dy, dc = split_slot(t)
        source = place(4 - dx, 4 - dy, dc)
        index = route[QUERY, source]
        expos, top, total, moment = softmax_part(
            [fin_k[t, :, lanes] for lanes in heads], [q_ref[index, :, lanes] for lanes in heads]
        )
        near_top, near_total, near_moment = near_stat[index, 0], near_stat[index, 1], near_stat[index, 2]
        bias = near_stat[index, 3]
        shifted = top + bias
        joint = jnp.maximum(near_top, shifted)
        near_weight, weight = jnp.exp(near_top - joint), jnp.exp(shifted - joint)
        denominator = near_total * near_weight + total * weight
        inverse = 1.0 / denominator
        near_weight, weight = near_weight * inverse, weight * inverse
        ent_slot[source] = (
            jnp.log(denominator) + joint - (near_moment * near_weight + (moment + bias * total) * weight)
        )
        shares = [
            jnp.concatenate(
                [near_expo[index, h] * near_weight[h : h + 1], expos[h] * weight[h : h + 1]], axis=0
            ).astype(jnp.bfloat16)
            for h in range(GROUP_HEADS)
        ]
        values = [
            jnp.concatenate([kv_ref[1, index, :, lanes], fin_v[t, :, lanes]], axis=0) for lanes in heads
        ]
        mixed = [
            lax.dot_general(p, v, (((0,), (0,)), ((), ())), preferred_element_type=F32) for p, v in zip(shares, values)
        ]
        for h, lanes in enumerate(heads):
            out_slot[source, :, lanes] = mixed[h].astype(jnp.bfloat16)

    def arrived(u, carry):
        t = nth_slot(u)

        @pl.when(t != 0)
        def _():
            second_k(t, True).wait_recv()
            second_v(t, True).wait_recv()

        attend(t)
        return carry

    lax.fori_loop(0, N_SEQ, arrived, 0)

    lane = lax.broadcasted_iota(jnp.int32, (GROUP_HEADS, 128), 1)
    entropy = jnp.zeros((GROUP_HEADS, 128), F32)
    for i in range(BLOCKS_DEV):
        source = route[OWNER, i]
        att_ref[i] = out_slot[source]
        mean = jnp.sum(ent_slot[source], axis=1, keepdims=True) * (1.0 / BLOCK)
        entropy = jnp.where(lane == i, mean, entropy)
    ent_ref[...] = entropy[:, :BLOCKS_DEV]

    for t in order:
        dx, dy, dc = split_slot(t)
        if dx:
            first_k(t, False).wait_send()
        if dy:
            first_v(t, False).wait_send()
        if not is_final_k(t):
            second_k(t, True).wait_send()
        if not is_final_v(t):
            second_v(t, True).wait_send()


def routes(chart):
    seq = lax.axis_index("seq")
    table = chart.reshape(N_SEQ, BLOCKS_DEV)
    wanted = jnp.sum(jnp.where(table // BLOCKS_DEV == seq, table % BLOCKS_DEV, 0), axis=1)
    own = lax.dynamic_index_in_dim(table, seq, 0, keepdims=False)
    owner = own // BLOCKS_DEV
    hit = jnp.arange(N_SEQ, dtype=jnp.int32)[:, None] == owner[None, :]
    query = jnp.sum(jnp.where(hit, jnp.arange(BLOCKS_DEV, dtype=jnp.int32)[None, :], 0), axis=1)
    return jnp.stack([wanted, query, jnp.concatenate([own, own]), jnp.concatenate([owner, owner])])


def on_device(queries, pile, softness, chart):
    slots = pltpu.VMEM((N_SEQ, BLOCK, WIDTH), jnp.bfloat16)
    dma = pltpu.SemaphoreType.DMA
    smem = pl.BlockSpec(memory_space=pltpu.SMEM)
    vmem = pl.BlockSpec(memory_space=pltpu.VMEM)
    attended, entropy = pl.pallas_call(
        kernel,
        out_shape=(
            jax.ShapeDtypeStruct((BLOCKS_DEV, BLOCK, WIDTH), jnp.bfloat16),
            jax.ShapeDtypeStruct((GROUP_HEADS, BLOCKS_DEV), F32),
        ),
        in_specs=[smem, smem, pl.BlockSpec(memory_space=pl.ANY), pl.BlockSpec(memory_space=pl.ANY)],
        out_specs=(vmem, vmem),
        scratch_shapes=[
            pltpu.VMEM((BLOCKS_DEV, BLOCK, WIDTH), jnp.bfloat16),
            pltpu.VMEM((2, BLOCKS_DEV, BLOCK, WIDTH), jnp.bfloat16),
            pltpu.VMEM((BLOCKS_DEV, GROUP_HEADS, BLOCK, BLOCK), F32),
            pltpu.VMEM((BLOCKS_DEV, 4, GROUP_HEADS, BLOCK), F32),
            slots, slots, slots, slots, slots, slots, slots,
            pltpu.VMEM((N_SEQ, GROUP_HEADS, 128), F32),
            pltpu.VMEM((64, WIDTH), F32),
            pltpu.VMEM((128, WIDTH), F32),
            pltpu.VMEM((N_HEADS, 8, 128), F32),
            pltpu.VMEM((N_HEADS, 8, 128), F32),
            pltpu.VMEM((N_HEADS, 8, 4, 8, 128), F32),
            pltpu.VMEM((N_HEADS, 8, 8, 128), F32),
            pltpu.VMEM((4, 8, 128), F32),
            pltpu.VMEM((BLOCKS_DEV, ALL_BLOCKS), F32),
            dma((3,)), dma((11,)), dma((11,)), dma((8,)), dma((8,)), dma((18,)), dma((18,)),
            dma((N_SEQ,)), dma((N_SEQ,)), dma((N_SEQ,)), dma((N_SEQ,)),
            dma((N_SEQ,)), dma((N_SEQ,)), dma((N_SEQ,)), dma((N_SEQ,)),
        ],
        compiler_params=pltpu.CompilerParams(
            collective_id=0, has_side_effects=True, vmem_limit_bytes=60 * 1024 * 1024
        ),
        name="sparse_attention",
    )(
        routes(chart), softness, queries.reshape(BLOCKS_DEV, BLOCK, WIDTH), pile.reshape(2, BLOCKS_DEV, BLOCK, WIDTH)
    )
    return attended.reshape(queries.shape), entropy


def solution(mesh):
    in_specs = (P("seq", "heads"), P(None, "seq", "heads"), P(), P("heads", None))
    out_specs = (P("seq", "heads"), P("heads", "seq"))
    return jax.shard_map(
        on_device, mesh=mesh, in_specs=in_specs, out_specs=out_specs, check_vma=False
    )
```

time: 163 us -> 128 us (0.79)
  Pallas kernels: 156 us -> 120 us
    pallas_call x1, Pallas kernels: 156 us -> 120 us  [on_device(): pl.pallas_call(kernel, out_shape=(jax.ShapeDtypeStruct((BLOCKS_DEV, BLOCK...]
where the time goes in v2:
time: 128 us; the launch traced here: 127 us
  Pallas kernels  120 us (94%)
  local copies, waits for them, and re-layouts  4.22 us (3%)
  other arithmetic  2.29 us (2%)
    pallas_call x1, Pallas kernels, on_device(): pl.pallas_call(kernel, out_shape=(jax.ShapeDtypeStruct((BLOCKS_DEV, BLOCK...  120 us
    unnamed x5, local copies, waits for them, and re-layouts  4.14 us

profile of v2, /device:TPU:1, one launch (start us, length us, event | category | flops | bytes accessed | tf_op | source)
XLA Modules:
  0.0 127.4 jit_solution(13292511628198367104)
XLA Ops:
  0.6 0.5 broadcast.87
  1.1 1.3 %reduce.3 = s32[512]{0:T(512)S(1)} reduce(s32[1,512]{1,0:T(1,128)} %param.7, s32[]{:T(128)} %broadcast.87), dimensions={0}, to_apply=%param.7.reduce_sub_computation.3 | reduce | bytes 4100 | tf_op args[3]
  2.5 0.1 reshape.16
  2.6 0.1 fusion.2
  2.7 0.1 select_reduce_fusion
  2.9 0.1 add_bitcast_fusion
  2.9 0.6 pad_add_fusion.route
  3.5 120.2 %sparse_attention.1 = (bf16[16,128,512]{2,1,0:T(8,128)(2,1)}, f32[4,16]{1,0:T(4,128)}) custom-call(s32[4,32]{1,0:T(4,128)} %pad_add_fusion.route, f32[8]{0:T(128)} %soft.1, bf16[16,128,512]{2,1,0:T(8,128)(2,1)} %bitcast.15, bf16[2,16,128,512]{3,2,1,0:T(8,128)(2,1)} %bitcast.14), custom_call_target="tpu_custom_call" | custom-call | tf_op jit(solution)/shard_map/sparse_attention/pallas_call | solution.py:355
  123.7 0.0 copy-start
  123.7 3.0 %copy.8 = bf16[2048,512]{1,0:T(8,128)(2,1)} copy(bf16[2048,512]{1,0:T(8,128)(2,1)} %bitcast.16) | data formatting | bytes 4194304
  126.8 0.0 copy-done
  126.8 0.6 copy.9
  (2 shorter events, 0.0 us)
Async XLA Ops:
  123.7 3.1 %copy-start = (f32[4,16]{1,0:T(4,128)S(1)}, f32[4,16]{1,0:T(4,128)}, u32[]{:S(2)}) copy-start(f32[4,16]{1,0:T(4,128)} %get-tuple-element.13) | copy-start | bytes 772

commit v3 on v2

--- a/solution.py
+++ b/solution.py
@@ -22,7 +22,6 @@
 PRICE = 1.0 / (BLOCK * math.sqrt(HEAD_DIM * HEADS))
 SCALE = HEAD_DIM ** (-0.5)
 LOG2E = math.log2(math.e)
-WANTED, QUERY, PARTNER, OWNER = range(4)
 
 
 def split_slot(t):
@@ -30,10 +29,10 @@
 
 
 def kernel(
-    route, soft, q_hbm, kv_hbm, att_ref, ent_ref, q_ref, kv_ref, near_expo, near_stat,
-    pack_k, pack_v, mid_k, mid_v, fin_k, fin_v, out_slot, ent_slot,
+    chart, soft, q_hbm, kv_hbm, att_hbm, ent_slot, q_ref, k_ref, v_ref, near_expo, near_stat,
+    pack_k, pack_v, mid_k, mid_v, fin_k, fin_v, out_slot,
     q_sum, k_sum, part, part_in, cost, row_pot, col_pot, mine,
-    load_sem, sum_send, sum_recv, red_send, red_recv, tile_send, tile_recv,
+    load_sem, out_sem, sum_send, sum_recv, red_send, red_recv, tile_send, tile_recv,
     first_k_send, first_v_send, mid_k_recv, mid_v_recv,
     second_k_send, second_v_send, fin_k_recv, fin_v_recv,
 ):
@@ -56,12 +55,12 @@
             src_ref=src, dst_ref=dst, send_sem=send, recv_sem=recv, device_id=to, device_id_type=MESH
         )
 
-    load_k = pltpu.make_async_copy(kv_hbm.at[0], kv_ref.at[0], load_sem.at[0])
+    load_k = pltpu.make_async_copy(kv_hbm.at[0], k_ref, load_sem.at[0])
     load_q = pltpu.make_async_copy(q_hbm, q_ref, load_sem.at[1])
-    load_v = pltpu.make_async_copy(kv_hbm.at[1], kv_ref.at[1], load_sem.at[2])
+    load_v = pltpu.make_async_copy(kv_hbm.at[1], v_ref, load_sem.at[2])
     load_k.start()
+    load_v.start()
     load_q.start()
-    load_v.start()
     barrier = pltpu.get_barrier_semaphore()
     peers = [device(d, 0, e) for d in (1, 2, 3) for e in (0, 1)]
     peers += [device(0, d, e) for d in (1, 2, 3) for e in (0, 1)]
@@ -69,15 +68,76 @@
     for peer in peers:
         pl.semaphore_signal(barrier, inc=1, device_id=peer, device_id_type=MESH)
 
+    def first_k(t, final):
+        dst, recv = (fin_k, fin_k_recv) if final else (mid_k, mid_k_recv)
+        return remote(pack_k.at[t], dst.at[t], first_k_send.at[t], recv.at[t], device(t // 8, 0, 0))
+
+    def first_v(t, final):
+        dst, recv = (fin_v, fin_v_recv) if final else (mid_v, mid_v_recv)
+        return remote(pack_v.at[t], dst.at[t], first_v_send.at[t], recv.at[t], device(0, (t // 2) % 4, 0))
+
+    def second_k(t, direct):
+        src = pack_k if direct else mid_k
+        _, dy, dc = split_slot(t)
+        return remote(src.at[t], fin_k.at[t], second_k_send.at[t], fin_k_recv.at[t], device(0, dy, dc))
+
+    def second_v(t, direct):
+        src = pack_v if direct else mid_v
+        dx, _, dc = split_slot(t)
+        return remote(src.at[t], fin_v.at[t], second_v_send.at[t], fin_v_recv.at[t], device(dx, 0, dc))
+
+    def is_final_k(t):
+        return t % 8 == 0
+
+    def is_final_v(t):
+        return t // 8 == 0 and t % 2 == 0
+
+    def nth_slot(u):
+        j = (u // 2) % 4
+        return ((j + 1) % 4) * 8 + ((j + u // 8 + 1) % 4) * 2 + u % 2
+
+    order = [nth_slot(u) for u in range(N_SEQ)]
+
+    def wanted(t):
+        first = place(*split_slot(t)) * BLOCKS_DEV
+        index = jnp.int32(0)
+        for i in range(BLOCKS_DEV):
+            entry = chart[0, first + i]
+            index = jnp.maximum(index, jnp.where(entry >> 4 == seq, entry & (BLOCKS_DEV - 1), 0))
+        return index
+
+    def send_k(t, index):
+        into = pack_k if t else fin_k
+        into[t] = k_ref[index]
+        if t // 8:
+            first_k(t, is_final_k(t)).start()
+
+    def send_v(t, index):
+        into = pack_v if t else fin_v
+        into[t] = v_ref[index]
+        if (t // 2) % 4:
+            first_v(t, is_final_v(t)).start()
+
+    def send_slots(slots):
+        for t in slots:
+            index = wanted(t)
+            send_k(t, index)
+            send_v(t, index)
+
+    load_k.wait()
+    pl.semaphore_wait(barrier, len(peers))
+    early = [(t, wanted(t)) for t in order[:4]]
+    for t, index in early:
+        send_k(t, index)
+    load_v.wait()
+    for t, index in early:
+        send_v(t, index)
+
     q_rows = pl.ds(pl.multiple_of(x * BLOCKS_DEV, BLOCKS_DEV), BLOCKS_DEV)
     k_rows = pl.ds(pl.multiple_of(yc * BLOCKS_DEV, BLOCKS_DEV), BLOCKS_DEV)
-    load_k.wait()
-    k_sum[k_rows, :] = jnp.sum(kv_ref[0].astype(F32), axis=1)
+    k_sum[k_rows, :] = jnp.sum(k_ref[...].astype(F32), axis=1)
     load_q.wait()
     q_sum[q_rows, :] = jnp.sum(q_ref[...].astype(F32), axis=1)
-
-    pl.semaphore_wait(barrier, len(peers))
-
     sums = []
     for d in (1, 2, 3):
         sums.append(remote(q_sum.at[q_rows], q_sum.at[q_rows], sum_send.at[d], sum_recv.at[d], device(d, 0, 0)))
@@ -87,52 +147,19 @@
         )
     for copy in sums:
         copy.start()
-
-    def first_k(t, final):
-        dst, recv = (fin_k, fin_k_recv) if final else (mid_k, mid_k_recv)
-        return remote(pack_k.at[t], dst.at[t], first_k_send.at[t], recv.at[t], device(t // 8, 0, 0))
-
-    def first_v(t, final):
-        dst, recv = (fin_v, fin_v_recv) if final else (mid_v, mid_v_recv)
-        return remote(pack_v.at[t], dst.at[t], first_v_send.at[t], recv.at[t], device(0, (t // 2) % 4, 0))
-
-    def second_k(t, direct):
-        src = pack_k if direct else mid_k
-        _, dy, dc = split_slot(t)
-        return remote(src.at[t], fin_k.at[t], second_k_send.at[t], fin_k_recv.at[t], device(0, dy, dc))
-
-    def second_v(t, direct):
-        src = pack_v if direct else mid_v
-        dx, _, dc = split_slot(t)
-        return remote(src.at[t], fin_v.at[t], second_v_send.at[t], fin_v_recv.at[t], device(dx, 0, dc))
-
-    def is_final_k(t):
-        return t % 8 == 0
-
-    def is_final_v(t):
-        return t // 8 == 0 and t % 2 == 0
-
-    def nth_slot(u):
-        j = (u // 2) % 4
-        return ((j + 1) % 4) * 8 + ((j + u // 8 + 1) % 4) * 2 + u % 2
-
-    order = [nth_slot(u) for u in range(N_SEQ)]
-
-    def fill_k(t, into):
-        into[t] = kv_ref[0, route[WANTED, place(*split_slot(t))]]
-
-    def fill_v(t, into):
-        into[t] = kv_ref[1, route[WANTED, place(*split_slot(t))]]
-
-    load_v.wait()
-    for t in order:
-        dx, dy, dc = split_slot(t)
-        fill_k(t, pack_k if t else fin_k)
-        if dx:
-            first_k(t, is_final_k(t)).start()
-        fill_v(t, pack_v if t else fin_v)
-        if dy:
-            first_v(t, is_final_v(t)).start()
+    send_slots(order[4:12])
+
+    def pass_slots(slots):
+        for t in slots:
+            dx, dy, dc = split_slot(t)
+            if dx and not is_final_k(t):
+                first_k(t, False).wait_recv()
+            if not is_final_k(t):
+                second_k(t, dx == 0).start()
+            if dy and not is_final_v(t):
+                first_v(t, False).wait_recv()
+            if not is_final_v(t):
+                second_v(t, dy == 0).start()
 
     turned = (((1,), (1,)), ((), ()))
 
@@ -149,7 +176,7 @@
 
     def near_part(i):
         expos, top, total, moment = softmax_part(
-            [kv_ref[0, i, :, lanes] for lanes in heads], [q_ref[i, :, lanes] for lanes in heads]
+            [k_ref[i, :, lanes] for lanes in heads], [q_ref[i, :, lanes] for lanes in heads]
         )
         for h in range(GROUP_HEADS):
             near_expo[i, h] = expos[h]
@@ -177,6 +204,7 @@
     for copy in reduces:
         copy.start()
     part_in[z] = part[z]
+    send_slots(order[12:20])
     near_parts(0)
     for copy in reduces:
         copy.wait()
@@ -187,6 +215,7 @@
         tiles.append(remote(tile, tile, tile_send.at[d], tile_recv.at[d], device(d, 0, 0)))
     for copy in tiles:
         copy.start()
+    send_slots(order[20:])
     near_parts(4)
     for copy in tiles:
         copy.wait()
@@ -196,29 +225,29 @@
         tiles.append(remote(strip, strip, tile_send.at[3 + r], tile_recv.at[3 + r], device(0, r // 2, r % 2)))
     for copy in tiles:
         copy.start()
+    pass_slots(order[:8])
     near_parts(8)
     for copy in tiles:
         copy.wait()
+    half_layer = pl.ds(c * 4, 4)
     tiles = []
     for d in range(1, N_HEADS):
-        layer = cost.at[z]
+        layer = cost.at[z, half_layer]
         tiles.append(remote(layer, layer, tile_send.at[10 + d], tile_recv.at[10 + d], floor(d)))
     for copy in tiles:
         copy.start()
 
     near_parts(12)
-    for t in order:
-        dx, dy, dc = split_slot(t)
-        if dx and not is_final_k(t):
-            first_k(t, False).wait_recv()
-        if not is_final_k(t):
-            second_k(t, dx == 0).start()
-        if dy and not is_final_v(t):
-            first_v(t, False).wait_recv()
-        if not is_final_v(t):
-            second_v(t, dy == 0).start()
-
-    for copy in tiles:
+    pass_slots(order[8:20])
+    handed = []
+    for d in range(1, N_HEADS):
+        tiles[d - 1].wait()
+        layer = cost.at[lax.rem(z + N_HEADS - d, N_HEADS), half_layer]
+        copy = remote(layer, layer, tile_send.at[17 + d], tile_recv.at[17 + d], device(0, 0, 1))
+        copy.start()
+        handed.append(copy)
+    pass_slots(order[20:])
+    for copy in handed:
         copy.wait()
 
     col_pot[...] = jnp.zeros_like(col_pot)
@@ -262,17 +291,22 @@
     queries = lax.broadcasted_iota(jnp.int32, (BLOCKS_DEV, 128), 0)
     partner = jnp.zeros((BLOCKS_DEV, 128), jnp.int32)
     for i in range(BLOCKS_DEV):
-        partner = jnp.where(queries == i, route[PARTNER, i], partner)
+        partner = jnp.where(queries == i, chart[0, seq * BLOCKS_DEV + i], partner)
     partner = jnp.concatenate([partner] * 4, axis=1)
     columns = lax.broadcasted_iota(jnp.int32, (BLOCKS_DEV, ALL_BLOCKS), 1)
     biases = jnp.sum(jnp.where(columns == partner, mine[...], 0.0), axis=1, keepdims=True)
     for i in range(BLOCKS_DEV):
         near_stat[i, 3] = jnp.broadcast_to(biases[i : i + 1], (GROUP_HEADS, 128))
 
+    def store(source):
+        return pltpu.make_async_copy(out_slot.at[source], att_hbm.at[source], out_sem.at[source])
+
     def attend(t):
         dx, dy, dc = split_slot(t)
         source = place(4 - dx, 4 - dy, dc)
-        index = route[QUERY, source]
+        index = jnp.int32(0)
+        for i in range(BLOCKS_DEV):
+            index = jnp.maximum(index, jnp.where(chart[0, seq * BLOCKS_DEV + i] >> 4 == source, i, 0))
         expos, top, total, moment = softmax_part(
             [fin_k[t, :, lanes] for lanes in heads], [q_ref[index, :, lanes] for lanes in heads]
         )
@@ -294,13 +328,14 @@
             for h in range(GROUP_HEADS)
         ]
         values = [
-            jnp.concatenate([kv_ref[1, index, :, lanes], fin_v[t, :, lanes]], axis=0) for lanes in heads
+            jnp.concatenate([v_ref[index, :, lanes], fin_v[t, :, lanes]], axis=0) for lanes in heads
         ]
         mixed = [
             lax.dot_general(p, v, (((0,), (0,)), ((), ())), preferred_element_type=F32) for p, v in zip(shares, values)
         ]
         for h, lanes in enumerate(heads):
             out_slot[source, :, lanes] = mixed[h].astype(jnp.bfloat16)
+        store(source).start()
 
     def arrived(u, carry):
         t = nth_slot(u)
@@ -315,14 +350,11 @@
 
     lax.fori_loop(0, N_SEQ, arrived, 0)
 
-    lane = lax.broadcasted_iota(jnp.int32, (GROUP_HEADS, 128), 1)
-    entropy = jnp.zeros((GROUP_HEADS, 128), F32)
-    for i in range(BLOCKS_DEV):
-        source = route[OWNER, i]
-        att_ref[i] = out_slot[source]
-        mean = jnp.sum(ent_slot[source], axis=1, keepdims=True) * (1.0 / BLOCK)
-        entropy = jnp.where(lane == i, mean, entropy)
-    ent_ref[...] = entropy[:, :BLOCKS_DEV]
+    def stored(source, carry):
+        store(source).wait()
+        return carry
+
+    lax.fori_loop(0, N_SEQ, stored, 0)
 
     for t in order:
         dx, dy, dc = split_slot(t)
@@ -336,15 +368,24 @@
             second_v(t, True).wait_send()
 
 
-def routes(chart):
-    seq = lax.axis_index("seq")
-    table = chart.reshape(N_SEQ, BLOCKS_DEV)
-    wanted = jnp.sum(jnp.where(table // BLOCKS_DEV == seq, table % BLOCKS_DEV, 0), axis=1)
-    own = lax.dynamic_index_in_dim(table, seq, 0, keepdims=False)
-    owner = own // BLOCKS_DEV
-    hit = jnp.arange(N_SEQ, dtype=jnp.int32)[:, None] == owner[None, :]
-    query = jnp.sum(jnp.where(hit, jnp.arange(BLOCKS_DEV, dtype=jnp.int32)[None, :], 0), axis=1)
-    return jnp.stack([wanted, query, jnp.concatenate([own, own]), jnp.concatenate([owner, owner])])
+def in_query_order(chart, att_slot, ent_slot, att_hbm, ent_ref, held, in_sem, out_sem):
+    first = lax.axis_index("seq") * BLOCKS_DEV
+    sources = [chart[0, first + i] >> 4 for i in range(BLOCKS_DEV)]
+    copies = [pltpu.make_async_copy(att_slot.at[source], held.at[i], in_sem.at[i]) for i, source in enumerate(sources)]
+    stores = [pltpu.make_async_copy(held.at[i], att_hbm.at[i], out_sem.at[i]) for i in range(BLOCKS_DEV)]
+    for copy in copies:
+        copy.start()
+    lane = lax.broadcasted_iota(jnp.int32, (GROUP_HEADS, 128), 1)
+    entropy = jnp.zeros((GROUP_HEADS, 128), F32)
+    for i, source in enumerate(sources):
+        mean = jnp.sum(ent_slot[source], axis=1, keepdims=True) * (1.0 / BLOCK)
+        entropy = jnp.where(lane == i, mean, entropy)
+    ent_ref[...] = entropy[:, :BLOCKS_DEV]
+    for copy, store in zip(copies, stores):
+        copy.wait()
+        store.start()
+    for store in stores:
+        store.wait()
 
 
 def on_device(queries, pile, softness, chart):
@@ -352,21 +393,22 @@
     dma = pltpu.SemaphoreType.DMA
     smem = pl.BlockSpec(memory_space=pltpu.SMEM)
     vmem = pl.BlockSpec(memory_space=pltpu.VMEM)
-    attended, entropy = pl.pallas_call(
+    hbm = pl.BlockSpec(memory_space=pl.ANY)
+    att_slot, ent_slot = pl.pallas_call(
         kernel,
         out_shape=(
-            jax.ShapeDtypeStruct((BLOCKS_DEV, BLOCK, WIDTH), jnp.bfloat16),
-            jax.ShapeDtypeStruct((GROUP_HEADS, BLOCKS_DEV), F32),
+            jax.ShapeDtypeStruct((N_SEQ, BLOCK, WIDTH), jnp.bfloat16),
+            jax.ShapeDtypeStruct((N_SEQ, GROUP_HEADS, BLOCK), F32),
         ),
-        in_specs=[smem, smem, pl.BlockSpec(memory_space=pl.ANY), pl.BlockSpec(memory_space=pl.ANY)],
-        out_specs=(vmem, vmem),
+        in_specs=[smem, smem, hbm, hbm],
+        out_specs=(hbm, vmem),
         scratch_shapes=[
             pltpu.VMEM((BLOCKS_DEV, BLOCK, WIDTH), jnp.bfloat16),
-            pltpu.VMEM((2, BLOCKS_DEV, BLOCK, WIDTH), jnp.bfloat16),
+            pltpu.VMEM((BLOCKS_DEV, BLOCK, WIDTH), jnp.bfloat16),
+            pltpu.VMEM((BLOCKS_DEV, BLOCK, WIDTH), jnp.bfloat16),
             pltpu.VMEM((BLOCKS_DEV, GROUP_HEADS, BLOCK, BLOCK), F32),
             pltpu.VMEM((BLOCKS_DEV, 4, GROUP_HEADS, BLOCK), F32),
             slots, slots, slots, slots, slots, slots, slots,
-            pltpu.VMEM((N_SEQ, GROUP_HEADS, 128), F32),
             pltpu.VMEM((64, WIDTH), F32),
             pltpu.VMEM((128, WIDTH), F32),
             pltpu.VMEM((N_HEADS, 8, 128), F32),
@@ -375,7 +417,7 @@
             pltpu.VMEM((N_HEADS, 8, 8, 128), F32),
             pltpu.VMEM((4, 8, 128), F32),
             pltpu.VMEM((BLOCKS_DEV, ALL_BLOCKS), F32),
-            dma((3,)), dma((11,)), dma((11,)), dma((8,)), dma((8,)), dma((18,)), dma((18,)),
+            dma((3,)), dma((N_SEQ,)), dma((11,)), dma((11,)), dma((8,)), dma((8,)), dma((25,)), dma((25,)),
             dma((N_SEQ,)), dma((N_SEQ,)), dma((N_SEQ,)), dma((N_SEQ,)),
             dma((N_SEQ,)), dma((N_SEQ,)), dma((N_SEQ,)), dma((N_SEQ,)),
         ],
@@ -384,8 +426,19 @@
         ),
         name="sparse_attention",
     )(
-        routes(chart), softness, queries.reshape(BLOCKS_DEV, BLOCK, WIDTH), pile.reshape(2, BLOCKS_DEV, BLOCK, WIDTH)
+        chart, softness, queries.reshape(BLOCKS_DEV, BLOCK, WIDTH), pile.reshape(2, BLOCKS_DEV, BLOCK, WIDTH)
     )
+    attended, entropy = pl.pallas_call(
+        in_query_order,
+        out_shape=(
+            jax.ShapeDtypeStruct((BLOCKS_DEV, BLOCK, WIDTH), jnp.bfloat16),
+            jax.ShapeDtypeStruct((GROUP_HEADS, BLOCKS_DEV), F32),
+        ),
+        in_specs=[smem, hbm, vmem],
+        out_specs=(hbm, vmem),
+        scratch_shapes=[pltpu.VMEM((BLOCKS_DEV, BLOCK, WIDTH), jnp.bfloat16), dma((BLOCKS_DEV,)), dma((BLOCKS_DEV,))],
+        name="query_order",
+    )(chart, att_slot, ent_slot)
     return attended.reshape(queries.shape), entropy
 
 

time: 128 us -> 118 us (0.922)
  local copies, waits for them, and re-layouts: 4.22 us -> 0 us
  Pallas kernels: 120 us -> 117 us
  other arithmetic: 2.29 us -> 0 us
    unnamed x5 -> x0, local copies, waits for them, and re-layouts: 4.14 us -> none
    pallas_call x1 -> x2, Pallas kernels: 120 us -> 117 us  [the longest x1 113 us: on_device(): pl.pallas_call(kernel, out_shape=(jax.ShapeDtypeStruct((N_SEQ, BLOCK, WID...]
    unnamed x1 -> x0, other arithmetic: 1.34 us -> none
where the time goes in v3:
time: 118 us
  Pallas kernels  117 us (99%)
    pallas_call x1, Pallas kernels, on_device(): pl.pallas_call(kernel, out_shape=(jax.ShapeDtypeStruct((N_SEQ, BLOCK, WID...  113 us
    pallas_call x1, Pallas kernels, on_device(): pl.pallas_call(in_query_order, out_shape=(jax.ShapeDtypeStruct((BLOCKS_DE...  4.03 us

profile of v3, /device:TPU:1, one launch (start us, length us, event | category | flops | bytes accessed | tf_op | source)
XLA Modules:
  0.0 117.7 jit_solution(5029596575463602666)
XLA Ops:
  0.6 113.0 %sparse_attention.1 = (bf16[32,128,512]{2,1,0:T(8,128)(2,1)}, f32[32,4,128]{2,1,0:T(4,128)}) custom-call(s32[1,512]{1,0:T(1,128)} %chart.3, f32[8]{0:T(128)} %soft.1, bf16[16,128,512]{2,1,0:T(8,128)(2,1)} %bitcast.4, bf16[2,16,128,512]{3,2,1,0:T(8,128)(2,1)} %bitcast.3), custom_call_target="tpu_custom_call" | custom-call | tf_op jit(solution)/shard_map/sparse_attention/pallas_call | solution.py:397
  113.6 4.0 %query_order.1 = (bf16[16,128,512]{2,1,0:T(8,128)(2,1)}, f32[4,16]{1,0:T(4,128)}) custom-call(s32[1,512]{1,0:T(1,128)} %chart.3, bf16[32,128,512]{2,1,0:T(8,128)(2,1)} %get-tuple-element.6.att_slot, f32[32,4,128]{2,1,0:T(4,128)} %get-tuple-element.7.ent_slot), custom_call_target="tpu_custom_call" | custom-call | tf_op jit(solution)/shard_map/query_order/pallas_call | solution.py:431

commit v4 on v3

--- a/solution.py
+++ b/solution.py
@@ -39,7 +39,7 @@
     seq = lax.axis_index("seq")
     z = lax.axis_index("heads")
     x, y, c = seq // 8, (seq // 2) % 4, seq % 2
-    yc = seq % 8
+    strip = c * 4 + y
 
     def place(dx, dy, dc):
         return lax.rem(x + dx, 4) * 8 + lax.rem(y + dy, 4) * 2 + lax.rem(c + dc, 2)
@@ -134,19 +134,26 @@
         send_v(t, index)
 
     q_rows = pl.ds(pl.multiple_of(x * BLOCKS_DEV, BLOCKS_DEV), BLOCKS_DEV)
-    k_rows = pl.ds(pl.multiple_of(yc * BLOCKS_DEV, BLOCKS_DEV), BLOCKS_DEV)
+
+    def k_rows_from(d):
+        return pl.ds(pl.multiple_of((lax.rem(y + 4 - d, 4) * 2 + c) * BLOCKS_DEV, BLOCKS_DEV), BLOCKS_DEV)
+
+    def to_other_core(d):
+        rows = k_rows_from(d)
+        return remote(k_sum.at[rows], k_sum.at[rows], sum_send.at[7 + d], sum_recv.at[7 + d], device(0, 0, 1))
+
+    k_rows = k_rows_from(0)
     k_sum[k_rows, :] = jnp.sum(k_ref[...].astype(F32), axis=1)
     load_q.wait()
     q_sum[q_rows, :] = jnp.sum(q_ref[...].astype(F32), axis=1)
     sums = []
     for d in (1, 2, 3):
         sums.append(remote(q_sum.at[q_rows], q_sum.at[q_rows], sum_send.at[d], sum_recv.at[d], device(d, 0, 0)))
-    for r in range(1, 8):
-        sums.append(
-            remote(k_sum.at[k_rows], k_sum.at[k_rows], sum_send.at[3 + r], sum_recv.at[3 + r], device(0, r // 2, r % 2))
-        )
+    for d in (1, 2, 3):
+        sums.append(remote(k_sum.at[k_rows], k_sum.at[k_rows], sum_send.at[3 + d], sum_recv.at[3 + d], device(0, d, 0)))
     for copy in sums:
         copy.start()
+    to_other_core(0).start()
     send_slots(order[4:12])
 
     def pass_slots(slots):
@@ -191,8 +198,14 @@
 
         lax.fori_loop(0, 4, step, 0)
 
-    for copy in sums:
-        copy.wait()
+    for d in (1, 2, 3):
+        sums[2 + d].wait()
+        to_other_core(d).start()
+    for copy in sums[:3]:
+        copy.wait()
+    send_slots(order[12:16])
+    for d in range(4):
+        to_other_core(d).wait()
     shares = lax.dot_general(
         q_sum[...], k_sum[...], (((1,), (1,)), ((), ())), precision=lax.Precision.HIGHEST, preferred_element_type=F32
     )
@@ -204,14 +217,14 @@
     for copy in reduces:
         copy.start()
     part_in[z] = part[z]
-    send_slots(order[12:20])
+    send_slots(order[16:20])
     near_parts(0)
     for copy in reduces:
         copy.wait()
-    cost[z, yc, x] = jnp.sum(part_in[...], axis=0)
+    cost[z, strip, x] = jnp.sum(part_in[...], axis=0)
     tiles = []
     for d in (1, 2, 3):
-        tile = cost.at[z, yc, x]
+        tile = cost.at[z, strip, x]
         tiles.append(remote(tile, tile, tile_send.at[d], tile_recv.at[d], device(d, 0, 0)))
     for copy in tiles:
         copy.start()
@@ -220,9 +233,9 @@
     for copy in tiles:
         copy.wait()
     tiles = []
-    for r in range(1, 8):
-        strip = cost.at[z, yc]
-        tiles.append(remote(strip, strip, tile_send.at[3 + r], tile_recv.at[3 + r], device(0, r // 2, r % 2)))
+    for d in (1, 2, 3):
+        tile = cost.at[z, strip]
+        tiles.append(remote(tile, tile, tile_send.at[3 + d], tile_recv.at[3 + d], device(0, d, 0)))
     for copy in tiles:
         copy.start()
     pass_slots(order[:8])
@@ -240,10 +253,11 @@
     near_parts(12)
     pass_slots(order[8:20])
     handed = []
-    for d in range(1, N_HEADS):
-        tiles[d - 1].wait()
+    for d in range(N_HEADS):
+        if d:
+            tiles[d - 1].wait()
         layer = cost.at[lax.rem(z + N_HEADS - d, N_HEADS), half_layer]
-        copy = remote(layer, layer, tile_send.at[17 + d], tile_recv.at[17 + d], device(0, 0, 1))
+        copy = remote(layer, layer, tile_send.at[18 + d], tile_recv.at[18 + d], device(0, 0, 1))
         copy.start()
         handed.append(copy)
     pass_slots(order[20:])
@@ -284,7 +298,7 @@
     inverse = LOG2E / soft[REFIT_REPEATS - 1]
     for half in range(2):
         k = x * 2 + half
-        coupling = (cost[k, yc] * inverse + row_pot[k, yc][None] + col_pot[...]) * math.log(2.0) + math.log(ALL_BLOCKS)
+        coupling = (cost[k, strip] * inverse + row_pot[k, strip][None] + col_pot[...]) * math.log(2.0) + math.log(ALL_BLOCKS)
         for column in range(4):
             mine[half * 8 : half * 8 + 8, column * 128 : column * 128 + 128] = coupling[column]
 
@@ -417,7 +431,7 @@
             pltpu.VMEM((N_HEADS, 8, 8, 128), F32),
             pltpu.VMEM((4, 8, 128), F32),
             pltpu.VMEM((BLOCKS_DEV, ALL_BLOCKS), F32),
-            dma((3,)), dma((N_SEQ,)), dma((11,)), dma((11,)), dma((8,)), dma((8,)), dma((25,)), dma((25,)),
+            dma((3,)), dma((N_SEQ,)), dma((11,)), dma((11,)), dma((8,)), dma((8,)), dma((26,)), dma((26,)),
             dma((N_SEQ,)), dma((N_SEQ,)), dma((N_SEQ,)), dma((N_SEQ,)),
             dma((N_SEQ,)), dma((N_SEQ,)), dma((N_SEQ,)), dma((N_SEQ,)),
         ],

time: 118 us -> 117 us (level)
  no operation moved by 1% of the time
where the time goes in v4:
time: 117 us
  Pallas kernels  116 us (99%)
    pallas_call x1, Pallas kernels, on_device(): pl.pallas_call(kernel, out_shape=(jax.ShapeDtypeStruct((N_SEQ, BLOCK, WID...  112 us
    pallas_call x1, Pallas kernels, on_device(): pl.pallas_call(in_query_order, out_shape=(jax.ShapeDtypeStruct((BLOCKS_DE...  4.03 us

profile of v4, /device:TPU:1, one launch (start us, length us, event | category | flops | bytes accessed | tf_op | source)
XLA Modules:
  0.0 117.0 jit_solution(12267663031012053307)
XLA Ops:
  0.6 112.3 %sparse_attention.1 = (bf16[32,128,512]{2,1,0:T(8,128)(2,1)}, f32[32,4,128]{2,1,0:T(4,128)}) custom-call(s32[1,512]{1,0:T(1,128)} %chart.3, f32[8]{0:T(128)} %soft.1, bf16[16,128,512]{2,1,0:T(8,128)(2,1)} %bitcast.4, bf16[2,16,128,512]{3,2,1,0:T(8,128)(2,1)} %bitcast.3), custom_call_target="tpu_custom_call" | custom-call | tf_op jit(solution)/shard_map/sparse_attention/pallas_call | solution.py:411
  113.0 4.0 %query_order.1 = (bf16[16,128,512]{2,1,0:T(8,128)(2,1)}, f32[4,16]{1,0:T(4,128)}) custom-call(s32[1,512]{1,0:T(1,128)} %chart.3, bf16[32,128,512]{2,1,0:T(8,128)(2,1)} %get-tuple-element.6.att_slot, f32[32,4,128]{2,1,0:T(4,128)} %get-tuple-element.7.ent_slot), custom_call_target="tpu_custom_call" | custom-call | tf_op jit(solution)/shard_map/query_order/pallas_call | solution.py:445
